TPU v7x, 32 devices: a whole 2x2x4 slice. The times are simulated.
32 devices in a mesh: hours: 2 (over x), chan: 2 (over core), freq: 8 (over z, y).
Axes of the slice: x: 2, y: 2, z: 4, core: 2. Of those that a mesh axis runs over, the one named last changes fastest.
Arguments:
- samples: bfloat16 [1152, 32, 1024], P('chan', ('hours', 'freq')), parts along dimension 1, may hold values from -18 to 18
Outputs:
- cross_spectra: bfloat16 [2, 256, 1152, 1152], P(None, ('hours', 'freq'), None, 'chan'), parts along dimension 1
There are 2 independent parts, one for each index of `hours`. A program takes and returns all parts, laid end to end along the dimension named above; each array names one. Nothing has to cross between parts.
All inputs are finite; a program needn't handle non-finite values.
Results may differ from a plain program's by a relative error of at most 0.008.
Values may be sent and summed in bfloat16 or wider, within the bound.
A program may use at most 192 MiB of HBM per device.

v0:
```python
import functools
import math

import jax
import jax.numpy as jnp
import numpy as np
from jax import lax
from jax.experimental import pallas as pl
from jax.experimental.pallas import tpu as pltpu
from jax.sharding import PartitionSpec as P

BINS = 128
LANES = 128
MESH = pl.DeviceIdType.MESH


def bin_table(length, bins):
    position = np.arange(length, dtype=np.int64)[:, None]
    number = np.arange(bins, dtype=np.int64)[None, :] + 1
    step = np.float32(2.0 * math.pi / length)
    phase = (position * number % length).astype(np.float32) * step
    half = np.float32(0.5)
    taper = half - half * np.cos(position.astype(np.float32) * step)
    factor = np.float32(math.sqrt(8.0 / (3.0 * length)))
    table = np.concatenate([taper * np.cos(phase), -(taper * np.sin(phase))], axis=1) * factor
    return jnp.asarray(table.astype(np.float32)).astype(jnp.bfloat16)


def whiten(real, imag):
    bins = real.shape[0]
    power = real * real + imag * imag
    row = lax.broadcasted_iota(jnp.int32, (bins, 1), 0)
    summed = power
    for shift in (1, 2):
        summed = summed + jnp.where(row >= shift, pltpu.roll(power, shift, 0), 0.0)
        summed = summed + jnp.where(row < bins - shift, pltpu.roll(power, bins - shift, 0), 0.0)
    count = jnp.minimum(row + 2, bins - 1) - jnp.maximum(row - 2, 0) + 1
    level = jnp.maximum(summed * (1.0 / count.astype(jnp.float32)), 0.1)
    scale = lax.rsqrt(level)
    return real * scale, imag * scale


def pack(real, imag):
    cut = real.shape[1] // LANES * LANES
    return jnp.concatenate([real[:, :cut], imag[:, :cut], real[:, cut:], imag[:, cut:]], axis=1)


def unpack(values, part, channels):
    cut = channels // LANES * LANES
    rest = channels - cut
    tail = 2 * cut + part * rest
    main = values[:, part * cut : (part + 1) * cut]
    return jnp.concatenate([main, values[:, tail : tail + rest]], axis=1) if rest else main


def exchange_kernel(count, spec_ref, own_ref, other_ref, white, send_sem, recv_sem, local_sem,
                    pass_sem, got_sem):
    hour = lax.axis_index("hours")
    chan = lax.axis_index("chan")
    me = lax.axis_index("freq")
    windows = spec_ref.shape[0]
    local_bins, width = own_ref.shape[1:]
    steps = sorted(range(1, count), key=lambda step: abs(2 * step - count))

    barrier = pltpu.get_barrier_semaphore()
    for step in steps:
        peer = lax.rem(me + step, count)
        pl.semaphore_signal(barrier, inc=1, device_id=(hour, chan, peer), device_id_type=MESH)
    pl.semaphore_signal(barrier, inc=1, device_id=(hour, 1 - chan, me), device_id_type=MESH)

    copies, passes = {}, []

    def block(owner):
        return own_ref.at[pl.ds(windows * owner, windows)]

    def forward(source_ref, owner, step):
        copy = pltpu.make_async_remote_copy(
            src_ref=source_ref,
            dst_ref=other_ref.at[pl.ds(windows * owner, windows)],
            send_sem=pass_sem.at[step],
            recv_sem=got_sem.at[step],
            device_id=(hour, 1 - chan, me),
            device_id_type=MESH,
        )
        copy.start()
        passes.append(copy)

    for w in range(windows):
        turned = spec_ref[w].T.astype(jnp.float32)
        real, imag = whiten(turned[:BINS], turned[BINS:])
        packed = pack(real, imag).astype(jnp.bfloat16)
        white[:, w] = packed.reshape(count, local_bins, width)
    pl.semaphore_wait(barrier, count)
    for step in steps:
        peer = lax.rem(me + step, count)
        copies[step] = pltpu.make_async_remote_copy(
            src_ref=white.at[peer],
            dst_ref=block(me),
            send_sem=send_sem.at[step],
            recv_sem=recv_sem.at[step],
            device_id=(hour, chan, peer),
            device_id_type=MESH,
        )
        copies[step].start()
    keep = pltpu.make_async_copy(white.at[me], block(me), local_sem)
    keep.start()
    forward(white.at[me], me, 0)
    for step in reversed(steps):
        copies[step].wait_recv()
        owner = lax.rem(me - step + count, count)
        forward(block(owner), owner, step)
    keep.wait()
    for copy in copies.values():
        copy.wait_send()
    for copy in passes:
        copy.wait()


def exchange(spec, count):
    windows, channels, _ = spec.shape
    local_bins = BINS // count
    shape = jax.ShapeDtypeStruct((windows * count, local_bins, 2 * channels), jnp.bfloat16)
    pieces = pltpu.SemaphoreType.DMA((count,))
    return pl.pallas_call(
        functools.partial(exchange_kernel, count),
        out_shape=(shape, shape),
        in_specs=[pl.BlockSpec(memory_space=pltpu.VMEM)],
        out_specs=(pl.BlockSpec(memory_space=pl.ANY), pl.BlockSpec(memory_space=pl.ANY)),
        scratch_shapes=[
            pltpu.VMEM((count, windows, local_bins, 2 * channels), jnp.bfloat16),
            pieces,
            pieces,
            pltpu.SemaphoreType.DMA,
            pieces,
            pieces,
        ],
        compiler_params=pltpu.CompilerParams(
            collective_id=0, has_side_effects=True, vmem_limit_bytes=40 << 20
        ),
        cost_estimate=pl.CostEstimate(
            flops=spec.size * 20, bytes_accessed=spec.size * 8, transcendentals=0
        ),
        name="exchange",
    )(spec)


def spread(tiles, first_row, values):
    height, width = values.shape
    for t in range(tiles.shape[0]):
        part = values[:, t * LANES : min((t + 1) * LANES, width)]
        if part.shape[1] < LANES:
            gap = jnp.zeros((height, LANES - part.shape[1]), part.dtype)
            part = jnp.concatenate([part, gap], axis=1)
        tiles[t, first_row : first_row + height] = part


def cross_kernel(scale, own_ref, other_ref, out_ref, mine, every):
    chan = lax.axis_index("chan")
    windows, local_bins, width = own_ref.shape
    channels = width // 2
    rows = windows * local_bins
    step_bins = out_ref.shape[1]
    step = pl.program_id(0)

    @pl.when(step == 0)
    def _():
        own = own_ref[...].astype(jnp.float32).reshape(rows, width)
        other = other_ref[...].astype(jnp.float32).reshape(rows, width)
        first = jnp.where(chan == 0, own, other)
        second = jnp.where(chan == 0, other, own)
        for part in range(2):
            spread(mine, part * rows, unpack(own, part, channels))
            pair = [unpack(first, part, channels), unpack(second, part, channels)]
            spread(every, part * rows, jnp.concatenate(pair, axis=1))

    for b in range(step_bins):
        pick = pl.ds(step * step_bins + b, 2 * windows, stride=local_bins)
        here = [mine[t, pick, :] for t in range(mine.shape[0])]
        here = jnp.concatenate(here, axis=1)[:, :channels]
        left = here.astype(jnp.bfloat16)
        swapped = jnp.concatenate([here[windows:], -here[:windows]], axis=0).astype(jnp.bfloat16)
        right = [every[t, pick, :].astype(jnp.bfloat16) for t in range(every.shape[0])]
        right = jnp.concatenate(right, axis=1)[:, :width]
        for part, side in ((0, left), (1, swapped)):
            product = lax.dot_general(
                side, right, (((0,), (0,)), ((), ())), preferred_element_type=jnp.float32
            )
            out_ref[part, b] = (product * scale).astype(jnp.bfloat16)


def cross(own, other):
    windows, local_bins, width = own.shape
    channels = width // 2
    rows = 2 * windows * local_bins
    step_bins = 2 if local_bins % 2 == 0 else 1
    shape = (2, local_bins, channels, width)
    whole = pl.BlockSpec(memory_space=pltpu.VMEM)
    return pl.pallas_call(
        functools.partial(cross_kernel, 1.0 / windows),
        grid=(local_bins // step_bins,),
        out_shape=jax.ShapeDtypeStruct(shape, jnp.bfloat16),
        in_specs=[whole, whole],
        out_specs=pl.BlockSpec((2, step_bins, channels, width), lambda k: (0, k, 0, 0)),
        scratch_shapes=[
            pltpu.VMEM((pl.cdiv(channels, LANES), rows, LANES), jnp.float32),
            pltpu.VMEM((pl.cdiv(width, LANES), rows, LANES), jnp.float32),
        ],
        compiler_params=pltpu.CompilerParams(vmem_limit_bytes=50 << 20),
        cost_estimate=pl.CostEstimate(
            flops=2 * rows * channels * width * 2,
            bytes_accessed=2 * math.prod(shape),
            transcendentals=0,
        ),
        name="cross",
    )(own, other)


def local(samples):
    length = samples.shape[2]
    table = bin_table(length, BINS)
    spec = jnp.einsum("cws,sj->wcj", samples, table, preferred_element_type=jnp.float32)
    own, other = exchange(spec.astype(jnp.bfloat16), lax.axis_size("freq"))
    return jnp.swapaxes(cross(own, other), 2, 3)


def solution(mesh):
    return jax.shard_map(
        local,
        mesh=mesh,
        in_specs=(P("chan", ("hours", "freq"), None),),
        out_specs=P(None, ("hours", "freq"), None, "chan"),
        check_vma=False,
    )
```

profile of v0, /device:TPU:15, one launch (start us, length us, event | category | flops | bytes accessed | tf_op | source)
XLA Modules:
  0.0 41.1 jit_solution(10116348869412288941)
XLA Ops:
  0.0 0.0 copy-start
  0.0 1.7 %copy-done = bf16[576,2,1024]{2,1,0:T(2,128)(2,1)S(1)} copy-done((bf16[576,2,1024]{2,1,0:T(2,128)(2,1)S(1)}, bf16[576,2,1024]{2,1,0:T(2,128)(2,1)}, u32[]{:S(2)}) %copy-start) | copy-done | bytes 2359320
  1.7 1.8 %fusion.5.spec_ref = bf16[2,576,256]{2,1,0:T(8,128)(2,1)S(1)} fusion(bf16[1024,256,1]{1,0,2:T(8,128)(2,1)} %constant.5, bf16[576,2,1024]{2,1,0:T(2,128)(2,1)S(1)} %copy-done), kind=kOutput, calls=%fused_computation.3 | convolution fusion | flops 604274688 | bytes 3473408 | tf_op jit(solution)/shard_map/cws,sj->wcj/dot_general | solution.py:221
  3.5 19.5 %exchange.1 = (bf16[16,16,1152]{2,1,0:T(8,128)(2,1)S(1)}, bf16[16,16,1152]{2,1,0:T(8,128)(2,1)S(1)}) custom-call(bf16[2,576,256]{2,1,0:T(8,128)(2,1)S(1)} %fusion.5.spec_ref), custom_call_target="tpu_custom_call" | custom-call | flops 5898240 | bytes 2359296 | tf_op jit(solution)/shard_map/exchange/pallas_call | solution.py:124
  23.0 18.1 %cross.1 = bf16[2,16,576,1152]{3,2,1,0:T(8,128)(2,1)} custom-call(bf16[16,16,1152]{2,1,0:T(8,128)(2,1)S(1)} %get-tuple-element.7.own_ref, bf16[16,16,1152]{2,1,0:T(8,128)(2,1)S(1)} %get-tuple-element.8.other_ref), custom_call_target="tpu_custom_call" | custom-call | flops 1358954496 | bytes 42467328 | tf_op jit(solution)/shard_map/cross/pallas_call | solution.py:198
Async XLA Ops:
  0.0 1.7 %copy-start = (bf16[576,2,1024]{2,1,0:T(2,128)(2,1)S(1)}, bf16[576,2,1024]{2,1,0:T(2,128)(2,1)}, u32[]{:S(2)}) copy-start(bf16[576,2,1024]{2,1,0:T(2,128)(2,1)} %param.2) | copy-start | bytes 7077892
where the time goes:
time: 41.3 us; the launch traced here: 41.1 us
  Pallas kernels  37.6 us (91%)
  matrix products  1.83 us (4%)
  local copies, waits for them, and re-layouts  1.67 us (4%)
    pallas_call x1, Pallas kernels, exchange(): pl.pallas_call(functools.partial(exchange_kernel, count), out_shape=(shap...  19.5 us
    pallas_call x1, Pallas kernels, cross(): pl.pallas_call(functools.partial(cross_kernel, 1.0 / windows), grid=(loca...  18.1 us
    dot_general x1, matrix products, local(): jnp.einsum('cws,sj->wcj', samples, table, preferred_element_type=jnp.floa...  1.83 us
    unnamed x2, local copies, waits for them, and re-layouts  1.67 us

commit v1 on v0

v1 whole, which is shorter than its diff:
```python
import functools
import math

import jax
import jax.numpy as jnp
import numpy as np
from jax import lax
from jax.experimental import pallas as pl
from jax.experimental.pallas import tpu as pltpu
from jax.sharding import PartitionSpec as P

BINS = 128
LANES = 128
MESH = pl.DeviceIdType.MESH


def bin_table(length, bins):
    position = np.arange(length, dtype=np.int64)[:, None]
    number = np.arange(bins, dtype=np.int64)[None, :] + 1
    step = np.float32(2.0 * math.pi / length)
    phase = (position * number % length).astype(np.float32) * step
    half = np.float32(0.5)
    taper = half - half * np.cos(position.astype(np.float32) * step)
    factor = np.float32(math.sqrt(8.0 / (3.0 * length)))
    table = np.concatenate([taper * np.cos(phase), -(taper * np.sin(phase))], axis=1) * factor
    return jnp.asarray(table.astype(np.float32)).astype(jnp.bfloat16)


def whiten(real, imag):
    bins = real.shape[0]
    power = real * real + imag * imag
    row = lax.broadcasted_iota(jnp.int32, (bins, 1), 0)
    summed = power
    for shift in (1, 2):
        summed = summed + jnp.where(row >= shift, pltpu.roll(power, shift, 0), 0.0)
        summed = summed + jnp.where(row < bins - shift, pltpu.roll(power, bins - shift, 0), 0.0)
    count = jnp.minimum(row + 2, bins - 1) - jnp.maximum(row - 2, 0) + 1
    level = jnp.maximum(summed * (1.0 / count.astype(jnp.float32)), 0.1)
    scale = lax.rsqrt(level)
    return real * scale, imag * scale


def chunks_of(channels):
    cut = channels // (2 * LANES) * LANES
    return ((0, cut), (cut, channels)) if cut else ((0, channels),)


def pack(real, imag):
    cut = real.shape[1] // LANES * LANES
    if cut == real.shape[1]:
        return jnp.concatenate([real, imag], axis=1)
    return jnp.concatenate([real[:, :cut], imag[:, :cut], real[:, cut:], imag[:, cut:]], axis=1)


def unpack(values, part):
    channels = values.shape[1] // 2
    cut = channels // LANES * LANES
    rest = channels - cut
    tail = 2 * cut + part * rest
    main = values[:, part * cut : (part + 1) * cut]
    return jnp.concatenate([main, values[:, tail : tail + rest]], axis=1) if rest else main


def spread(tiles, first_row, values):
    height, width = values.shape
    for t in range(pl.cdiv(width, LANES)):
        part = values[:, t * LANES : min((t + 1) * LANES, width)]
        if part.shape[1] < LANES:
            gap = jnp.zeros((height, LANES - part.shape[1]), part.dtype)
            part = jnp.concatenate([part, gap], axis=1)
        tiles[t, pl.ds(first_row, height), :] = part


def exchange_kernel(count, samples_ref, table_ref, mine_ref, every_ref, samples, table, flat, *rest):
    chunks = chunks_of(samples_ref.shape[0])
    n = len(chunks)
    white, own, other = rest[:n], rest[n : 2 * n], rest[2 * n : 3 * n]
    load_sem, send_sem, recv_sem, pass_sem, got_sem = rest[3 * n :]
    hour = lax.axis_index("hours")
    chan = lax.axis_index("chan")
    me = lax.axis_index("freq")
    windows = samples_ref.shape[1]
    local_bins = BINS // count
    rows = windows * local_bins
    total = rows * count
    scale = 1.0 / (windows * count)
    steps = sorted(range(1, count), key=lambda step: abs(2 * step - count))

    loads = [pltpu.make_async_copy(table_ref, table, load_sem.at[n])]
    for c, (low, high) in enumerate(chunks):
        here = pl.ds(low, high - low)
        loads.append(pltpu.make_async_copy(samples_ref.at[here], samples.at[here], load_sem.at[c]))
    for load in loads:
        load.start()

    barrier = pltpu.get_barrier_semaphore()
    for step in steps:
        peer = lax.rem(me + step, count)
        pl.semaphore_signal(barrier, inc=1, device_id=(hour, chan, peer), device_id_type=MESH)
    pl.semaphore_signal(barrier, inc=1, device_id=(hour, 1 - chan, me), device_id_type=MESH)

    sends, passes = {}, {}

    def forward(c, step, source_ref, owner):
        copy = pltpu.make_async_remote_copy(
            src_ref=source_ref,
            dst_ref=other[c].at[owner],
            send_sem=pass_sem.at[c, step],
            recv_sem=got_sem.at[c, step],
            device_id=(hour, 1 - chan, me),
            device_id_type=MESH,
        )
        copy.start()
        passes[c, step] = copy

    loads[0].wait()
    for c, (low, high) in enumerate(chunks):
        size = high - low
        loads[1 + c].wait()
        values = samples[low:high].reshape(size * windows, samples.shape[2])
        product = jnp.dot(values, table[...], preferred_element_type=jnp.float32)
        for part in range(2):
            flat[part, : size * windows] = product[:, part * BINS : (part + 1) * BINS]
        for w in range(windows):
            pick = pl.ds(w, size, stride=windows)
            real = flat[0, pick, :].astype(jnp.bfloat16).T.astype(jnp.float32)
            imag = flat[1, pick, :].astype(jnp.bfloat16).T.astype(jnp.float32)
            packed = pack(*whiten(real, imag)).astype(jnp.bfloat16)
            white[c][:, w] = packed.reshape(count, local_bins, 2 * size)
        if c == 0:
            pl.semaphore_wait(barrier, count)
        for step in steps:
            peer = lax.rem(me + step, count)
            copy = pltpu.make_async_remote_copy(
                src_ref=white[c].at[peer],
                dst_ref=own[c].at[me],
                send_sem=send_sem.at[c, step],
                recv_sem=recv_sem.at[c, step],
                device_id=(hour, chan, peer),
                device_id_type=MESH,
            )
            copy.start()
            sends[c, step] = copy
        forward(c, 0, white[c].at[me], me)

    def settle(step):
        owner = lax.rem(me - step + count, count)
        mine, theirs = [], []
        for c in range(n):
            width = white[c].shape[3]
            source = own[c] if step else white[c]
            passes[c, step].wait_recv()
            mine.append(source[owner].astype(jnp.float32).reshape(rows, width))
            theirs.append(other[c][owner].astype(jnp.float32).reshape(rows, width))
        for part in range(2):
            here = jnp.concatenate([unpack(x, part) for x in mine], axis=1)
            there = jnp.concatenate([unpack(x, part) for x in theirs], axis=1)
            first_row = pl.multiple_of(part * total + owner * rows, 8)
            spread(mine_ref, first_row, here * scale)
            pair = [jnp.where(chan == 0, here, there), jnp.where(chan == 0, there, here)]
            spread(every_ref, first_row, jnp.concatenate(pair, axis=1))

    waiting = [0]
    for step in reversed(steps):
        owner = lax.rem(me - step + count, count)
        for c in range(n):
            sends[c, step].wait_recv()
            forward(c, step, own[c].at[owner], owner)
        waiting.append(step)
        if len(waiting) > 2:
            settle(waiting.pop(0))
    for step in waiting:
        settle(step)
    for copy in sends.values():
        copy.wait_send()
    for copy in passes.values():
        copy.wait_send()


def exchange(samples, table, count):
    channels, windows, length = samples.shape
    local_bins = BINS // count
    rows = 2 * windows * count * local_bins
    chunks = chunks_of(channels)
    n = len(chunks)
    blocks = [
        pltpu.VMEM((count, windows, local_bins, 2 * (high - low)), jnp.bfloat16)
        for low, high in chunks
    ]
    largest = max(high - low for low, high in chunks)
    pieces = pltpu.SemaphoreType.DMA((n, count))
    whole = pl.BlockSpec(memory_space=pltpu.VMEM)
    return pl.pallas_call(
        functools.partial(exchange_kernel, count),
        out_shape=(
            jax.ShapeDtypeStruct((pl.cdiv(channels, LANES), rows, LANES), jnp.float32),
            jax.ShapeDtypeStruct((pl.cdiv(2 * channels, LANES), rows, LANES), jnp.float32),
        ),
        in_specs=[pl.BlockSpec(memory_space=pltpu.HBM), pl.BlockSpec(memory_space=pltpu.HBM)],
        out_specs=(whole, whole),
        scratch_shapes=[
            pltpu.VMEM(samples.shape, samples.dtype),
            pltpu.VMEM(table.shape, table.dtype),
            pltpu.VMEM((2, largest * windows, BINS), jnp.float32),
            *blocks,
            *blocks,
            *blocks,
            pltpu.SemaphoreType.DMA((n + 1,)),
            pieces,
            pieces,
            pieces,
            pieces,
        ],
        compiler_params=pltpu.CompilerParams(
            collective_id=0, has_side_effects=True, vmem_limit_bytes=40 << 20
        ),
        cost_estimate=pl.CostEstimate(
            flops=2 * samples.size * 2 * BINS, bytes_accessed=2 * samples.size, transcendentals=0
        ),
        name="exchange",
    )(samples, table)


def cross_kernel(mine_ref, every_ref, out_ref, held, sems):
    slots, step_bins, _, channels, width = held.shape
    step = pl.program_id(0)
    steps = out_ref.shape[1] // step_bins
    local_bins = steps * step_bins
    windows = mine_ref.shape[1] // (2 * local_bins)
    slot = lax.rem(step, slots)

    def copies(b, part, at_step, at_slot):
        return pltpu.make_async_copy(
            held.at[at_slot, b, part],
            out_ref.at[part, at_step * step_bins + b],
            sems.at[at_slot, b, part],
        )

    pieces = [(b, part) for b in range(step_bins) for part in range(2)]

    @pl.when(step >= slots)
    def _():
        for b, part in pieces:
            copies(b, part, step - slots, slot).wait()

    for b in range(step_bins):
        pick = pl.ds(step * step_bins + b, 2 * windows, stride=local_bins)
        here = [mine_ref[t, pick, :] for t in range(mine_ref.shape[0])]
        here = jnp.concatenate(here, axis=1)[:, :channels]
        left = here.astype(jnp.bfloat16)
        swapped = jnp.concatenate([here[windows:], -here[:windows]], axis=0).astype(jnp.bfloat16)
        right = [every_ref[t, pick, :].astype(jnp.bfloat16) for t in range(every_ref.shape[0])]
        right = jnp.concatenate(right, axis=1)[:, :width]
        for part, side in ((0, left), (1, swapped)):
            product = lax.dot_general(
                side, right, (((0,), (0,)), ((), ())), preferred_element_type=jnp.float32
            )
            held[slot, b, part] = product.astype(jnp.bfloat16)
            copies(b, part, step, slot).start()

    @pl.when(step == steps - 1)
    def _():
        for back in reversed(range(slots)):
            last = steps - 1 - back
            for b, part in pieces:
                copies(b, part, last, last % slots).wait()


def cross(mine, every, windows, channels):
    rows = mine.shape[1]
    local_bins = rows // (2 * windows)
    width = 2 * channels
    step_bins = 2 if local_bins % 2 == 0 else 1
    steps = local_bins // step_bins
    slots = min(2, steps)
    shape = (2, local_bins, channels, width)
    whole = pl.BlockSpec(memory_space=pltpu.VMEM)
    return pl.pallas_call(
        cross_kernel,
        grid=(steps,),
        out_shape=jax.ShapeDtypeStruct(shape, jnp.bfloat16),
        in_specs=[whole, whole],
        out_specs=pl.BlockSpec(memory_space=pl.ANY),
        scratch_shapes=[
            pltpu.VMEM((slots, step_bins, 2, channels, width), jnp.bfloat16),
            pltpu.SemaphoreType.DMA((slots, step_bins, 2)),
        ],
        compiler_params=pltpu.CompilerParams(vmem_limit_bytes=50 << 20),
        cost_estimate=pl.CostEstimate(
            flops=2 * rows * channels * width * 2,
            bytes_accessed=2 * math.prod(shape),
            transcendentals=0,
        ),
        name="cross",
    )(mine, every)


def local(samples):
    channels, windows, length = samples.shape
    count = lax.axis_size("freq")
    samples = pltpu.with_memory_space_constraint(samples, pltpu.HBM)
    table = pltpu.with_memory_space_constraint(bin_table(length, BINS), pltpu.HBM)
    mine, every = exchange(samples, table, count)
    return jnp.swapaxes(cross(mine, every, windows * count, channels), 2, 3)


def solution(mesh):
    return jax.shard_map(
        local,
        mesh=mesh,
        in_specs=(P("chan", ("hours", "freq"), None),),
        out_specs=P(None, ("hours", "freq"), None, "chan"),
        check_vma=False,
    )
```

time: 41.3 us -> 36.4 us (0.88)
  the two profiles are of different devices: /device:TPU:15 before, /device:TPU:1 now
where the time goes in v1:
time: 36.4 us; the launch traced here: 36 us
  Pallas kernels  36 us (99%)
    pallas_call x1, Pallas kernels, exchange(): pl.pallas_call(functools.partial(exchange_kernel, count), out_shape=(jax....  21.5 us
    pallas_call x1, Pallas kernels, cross(): pl.pallas_call(cross_kernel, grid=(steps,), out_shape=jax.ShapeDtypeStruc...  14.5 us

profile of v1, /device:TPU:1, one launch (start us, length us, event | category | flops | bytes accessed | tf_op | source)
XLA Modules:
  0.0 36.0 jit_solution(5959882814446412422)
XLA Ops:
  0.0 21.5 %exchange.1 = (f32[5,512,128]{2,1,0:T(8,128)S(1)}, f32[9,512,128]{2,1,0:T(8,128)S(1)}) custom-call(bf16[576,2,1024]{2,1,0:T(2,128)(2,1)} %samples_ref.1, bf16[1024,256]{1,0:T(8,128)(2,1)} %constant.4.table_ref), custom_call_target="tpu_custom_call" | custom-call | flops 603979776 | bytes 2359296 | tf_op jit(solution)/shard_map/exchange/pallas_call | solution.py:193
  21.5 14.5 %cross.1 = bf16[2,16,576,1152]{3,2,1,0:T(8,128)(2,1)} custom-call(f32[5,512,128]{2,1,0:T(8,128)S(1)} %get-tuple-element.7.mine_ref, f32[9,512,128]{2,1,0:T(8,128)S(1)} %get-tuple-element.8.every_ref), custom_call_target="tpu_custom_call" | custom-call | flops 1358954496 | bytes 42467328 | tf_op jit(solution)/shard_map/cross/pallas_call | solution.py:278

commit v2 on v1

--- a/solution.py
+++ b/solution.py
@@ -41,8 +41,20 @@
 
 
 def chunks_of(channels):
-    cut = channels // (2 * LANES) * LANES
-    return ((0, cut), (cut, channels)) if cut else ((0, channels),)
+    return ((0, LANES), (LANES, channels)) if channels > LANES else ((0, channels),)
+
+
+def order_of(count):
+    return sorted(range(1, count), key=lambda mask: (-mask.bit_length(), mask))
+
+
+def partner(me, mask, count):
+    bits = count.bit_length() - 1
+    other = 0
+    for bit in range(bits):
+        digit = lax.rem(me // (1 << bit), 2)
+        other = other + (1 << bit) * ((1 - digit) if mask >> bit & 1 else digit)
+    return other
 
 
 def pack(real, imag):
@@ -84,18 +96,19 @@
     rows = windows * local_bins
     total = rows * count
     scale = 1.0 / (windows * count)
-    steps = sorted(range(1, count), key=lambda step: abs(2 * step - count))
+    steps = order_of(count)
+    peers = {step: partner(me, step, count) for step in range(count)}
 
     loads = [pltpu.make_async_copy(table_ref, table, load_sem.at[n])]
     for c, (low, high) in enumerate(chunks):
         here = pl.ds(low, high - low)
         loads.append(pltpu.make_async_copy(samples_ref.at[here], samples.at[here], load_sem.at[c]))
-    for load in loads:
+    for load in loads[:2]:
         load.start()
 
     barrier = pltpu.get_barrier_semaphore()
     for step in steps:
-        peer = lax.rem(me + step, count)
+        peer = peers[step]
         pl.semaphore_signal(barrier, inc=1, device_id=(hour, chan, peer), device_id_type=MESH)
     pl.semaphore_signal(barrier, inc=1, device_id=(hour, 1 - chan, me), device_id_type=MESH)
 
@@ -113,7 +126,26 @@
         copy.start()
         passes[c, step] = copy
 
+    far = [step for step in steps if 2 * step >= count]
+    near = [step for step in steps if 2 * step < count]
+
+    def send(c, steps):
+        for step in steps:
+            peer = peers[step]
+            copy = pltpu.make_async_remote_copy(
+                src_ref=white[c].at[peer],
+                dst_ref=own[c].at[me],
+                send_sem=send_sem.at[c, step],
+                recv_sem=recv_sem.at[c, step],
+                device_id=(hour, chan, peer),
+                device_id_type=MESH,
+            )
+            copy.start()
+            sends[c, step] = copy
+
     loads[0].wait()
+    for load in loads[2:]:
+        load.start()
     for c, (low, high) in enumerate(chunks):
         size = high - low
         loads[1 + c].wait()
@@ -129,22 +161,14 @@
             white[c][:, w] = packed.reshape(count, local_bins, 2 * size)
         if c == 0:
             pl.semaphore_wait(barrier, count)
-        for step in steps:
-            peer = lax.rem(me + step, count)
-            copy = pltpu.make_async_remote_copy(
-                src_ref=white[c].at[peer],
-                dst_ref=own[c].at[me],
-                send_sem=send_sem.at[c, step],
-                recv_sem=recv_sem.at[c, step],
-                device_id=(hour, chan, peer),
-                device_id_type=MESH,
-            )
-            copy.start()
-            sends[c, step] = copy
+        send(c, far)
         forward(c, 0, white[c].at[me], me)
 
+    for c in range(n):
+        send(c, near)
+
     def settle(step):
-        owner = lax.rem(me - step + count, count)
+        owner = peers[step]
         mine, theirs = [], []
         for c in range(n):
             width = white[c].shape[3]
@@ -161,8 +185,8 @@
             spread(every_ref, first_row, jnp.concatenate(pair, axis=1))
 
     waiting = [0]
-    for step in reversed(steps):
-        owner = lax.rem(me - step + count, count)
+    for step in range(1, count):
+        owner = peers[step]
         for c in range(n):
             sends[c, step].wait_recv()
             forward(c, step, own[c].at[owner], owner)

time: 36.4 us -> 34.7 us (0.953)
  Pallas kernels: 36 us -> 34.6 us
    pallas_call x1, Pallas kernels: 21.5 us -> 20.1 us  [exchange(): pl.pallas_call(functools.partial(exchange_kernel, count), out_shape=(jax....]
where the time goes in v2:
time: 34.7 us; the launch traced here: 34.6 us
  Pallas kernels  34.6 us (100%)
    pallas_call x1, Pallas kernels, exchange(): pl.pallas_call(functools.partial(exchange_kernel, count), out_shape=(jax....  20.1 us
    pallas_call x1, Pallas kernels, cross(): pl.pallas_call(cross_kernel, grid=(steps,), out_shape=jax.ShapeDtypeStruc...  14.5 us

profile of v2, /device:TPU:1, one launch (start us, length us, event | category | flops | bytes accessed | tf_op | source)
XLA Modules:
  0.0 34.6 jit_solution(6346621890148127625)
XLA Ops:
  0.0 20.1 %exchange.1 = (f32[5,512,128]{2,1,0:T(8,128)S(1)}, f32[9,512,128]{2,1,0:T(8,128)S(1)}) custom-call(bf16[576,2,1024]{2,1,0:T(2,128)(2,1)} %samples_ref.1, bf16[1024,256]{1,0:T(8,128)(2,1)} %constant.4.table_ref), custom_call_target="tpu_custom_call" | custom-call | flops 603979776 | bytes 2359296 | tf_op jit(solution)/shard_map/exchange/pallas_call | solution.py:217
  20.1 14.5 %cross.1 = bf16[2,16,576,1152]{3,2,1,0:T(8,128)(2,1)} custom-call(f32[5,512,128]{2,1,0:T(8,128)S(1)} %get-tuple-element.7.mine_ref, f32[9,512,128]{2,1,0:T(8,128)S(1)} %get-tuple-element.8.every_ref), custom_call_target="tpu_custom_call" | custom-call | flops 1358954496 | bytes 42467328 | tf_op jit(solution)/shard_map/cross/pallas_call | solution.py:302

commit v3 on v2

--- a/solution.py
+++ b/solution.py
@@ -45,7 +45,7 @@
 
 
 def order_of(count):
-    return sorted(range(1, count), key=lambda mask: (-mask.bit_length(), mask))
+    return sorted(range(1, count), key=lambda mask: (-mask.bit_length(), mask ^ (mask >> 1 & 1)))
 
 
 def partner(me, mask, count):
@@ -83,11 +83,10 @@
         tiles[t, pl.ds(first_row, height), :] = part
 
 
-def exchange_kernel(count, samples_ref, table_ref, mine_ref, every_ref, samples, table, flat, *rest):
+def exchange_kernel(count, samples_ref, table_ref, mine_ref, every_ref, samples, table, flat,
+                    white, own, other, load_sem, send_sem, recv_sem, pass_sem, got_sem):
     chunks = chunks_of(samples_ref.shape[0])
     n = len(chunks)
-    white, own, other = rest[:n], rest[n : 2 * n], rest[2 * n : 3 * n]
-    load_sem, send_sem, recv_sem, pass_sem, got_sem = rest[3 * n :]
     hour = lax.axis_index("hours")
     chan = lax.axis_index("chan")
     me = lax.axis_index("freq")
@@ -114,27 +113,28 @@
 
     sends, passes = {}, {}
 
-    def forward(c, step, source_ref, owner):
+    def forward(step, source_ref, owner):
         copy = pltpu.make_async_remote_copy(
             src_ref=source_ref,
-            dst_ref=other[c].at[owner],
-            send_sem=pass_sem.at[c, step],
-            recv_sem=got_sem.at[c, step],
+            dst_ref=other.at[owner],
+            send_sem=pass_sem.at[step],
+            recv_sem=got_sem.at[step],
             device_id=(hour, 1 - chan, me),
             device_id_type=MESH,
         )
         copy.start()
-        passes[c, step] = copy
+        passes[step] = copy
 
     far = [step for step in steps if 2 * step >= count]
     near = [step for step in steps if 2 * step < count]
 
-    def send(c, steps):
+    def send(c, steps, low, high):
+        lanes = pl.ds(2 * low, 2 * (high - low))
         for step in steps:
             peer = peers[step]
             copy = pltpu.make_async_remote_copy(
-                src_ref=white[c].at[peer],
-                dst_ref=own[c].at[me],
+                src_ref=white.at[peer, :, :, lanes],
+                dst_ref=own.at[me, :, :, lanes],
                 send_sem=send_sem.at[c, step],
                 recv_sem=recv_sem.at[c, step],
                 device_id=(hour, chan, peer),
@@ -158,27 +158,24 @@
             real = flat[0, pick, :].astype(jnp.bfloat16).T.astype(jnp.float32)
             imag = flat[1, pick, :].astype(jnp.bfloat16).T.astype(jnp.float32)
             packed = pack(*whiten(real, imag)).astype(jnp.bfloat16)
-            white[c][:, w] = packed.reshape(count, local_bins, 2 * size)
+            white[:, w, :, 2 * low : 2 * high] = packed.reshape(count, local_bins, 2 * size)
         if c == 0:
             pl.semaphore_wait(barrier, count)
-        send(c, far)
-        forward(c, 0, white[c].at[me], me)
-
-    for c in range(n):
-        send(c, near)
+        send(c, far, low, high)
+    forward(0, white.at[me], me)
+    send(0, near, 0, samples_ref.shape[0])
 
     def settle(step):
         owner = peers[step]
-        mine, theirs = [], []
-        for c in range(n):
-            width = white[c].shape[3]
-            source = own[c] if step else white[c]
-            passes[c, step].wait_recv()
-            mine.append(source[owner].astype(jnp.float32).reshape(rows, width))
-            theirs.append(other[c][owner].astype(jnp.float32).reshape(rows, width))
+        passes[step].wait_recv()
+        source = own if step else white
+        mine = source[owner].astype(jnp.float32).reshape(rows, white.shape[3])
+        theirs = other[owner].astype(jnp.float32).reshape(rows, white.shape[3])
         for part in range(2):
-            here = jnp.concatenate([unpack(x, part) for x in mine], axis=1)
-            there = jnp.concatenate([unpack(x, part) for x in theirs], axis=1)
+            here, there = (
+                jnp.concatenate([unpack(x[:, 2 * a : 2 * b], part) for a, b in chunks], axis=1)
+                for x in (mine, theirs)
+            )
             first_row = pl.multiple_of(part * total + owner * rows, 8)
             spread(mine_ref, first_row, here * scale)
             pair = [jnp.where(chan == 0, here, there), jnp.where(chan == 0, there, here)]
@@ -188,8 +185,9 @@
     for step in range(1, count):
         owner = peers[step]
         for c in range(n):
-            sends[c, step].wait_recv()
-            forward(c, step, own[c].at[owner], owner)
+            if (c, step) in sends:
+                sends[c, step].wait_recv()
+        forward(step, own.at[owner], owner)
         waiting.append(step)
         if len(waiting) > 2:
             settle(waiting.pop(0))
@@ -207,10 +205,7 @@
     rows = 2 * windows * count * local_bins
     chunks = chunks_of(channels)
     n = len(chunks)
-    blocks = [
-        pltpu.VMEM((count, windows, local_bins, 2 * (high - low)), jnp.bfloat16)
-        for low, high in chunks
-    ]
+    blocks = pltpu.VMEM((count, windows, local_bins, 2 * channels), jnp.bfloat16)
     largest = max(high - low for low, high in chunks)
     pieces = pltpu.SemaphoreType.DMA((n, count))
     whole = pl.BlockSpec(memory_space=pltpu.VMEM)
@@ -226,14 +221,14 @@
             pltpu.VMEM(samples.shape, samples.dtype),
             pltpu.VMEM(table.shape, table.dtype),
             pltpu.VMEM((2, largest * windows, BINS), jnp.float32),
-            *blocks,
-            *blocks,
-            *blocks,
+            blocks,
+            blocks,
+            blocks,
             pltpu.SemaphoreType.DMA((n + 1,)),
             pieces,
             pieces,
-            pieces,
-            pieces,
+            pltpu.SemaphoreType.DMA((count,)),
+            pltpu.SemaphoreType.DMA((count,)),
         ],
         compiler_params=pltpu.CompilerParams(
             collective_id=0, has_side_effects=True, vmem_limit_bytes=40 << 20

time: 34.7 us -> 34.6 us (level)
  no operation moved by 1% of the time
where the time goes in v3:
time: 34.6 us; the launch traced here: 34.4 us
  Pallas kernels  34.4 us (99%)
    pallas_call x1, Pallas kernels, exchange(): pl.pallas_call(functools.partial(exchange_kernel, count), out_shape=(jax....  19.9 us
    pallas_call x1, Pallas kernels, cross(): pl.pallas_call(cross_kernel, grid=(steps,), out_shape=jax.ShapeDtypeStruc...  14.5 us

profile of v3, /device:TPU:1, one launch (start us, length us, event | category | flops | bytes accessed | tf_op | source)
XLA Modules:
  0.0 34.4 jit_solution(6748035961736545676)
XLA Ops:
  0.0 19.9 %exchange.1 = (f32[5,512,128]{2,1,0:T(8,128)S(1)}, f32[9,512,128]{2,1,0:T(8,128)S(1)}) custom-call(bf16[576,2,1024]{2,1,0:T(2,128)(2,1)} %samples_ref.1, bf16[1024,256]{1,0:T(8,128)(2,1)} %constant.4.table_ref), custom_call_target="tpu_custom_call" | custom-call | flops 603979776 | bytes 2359296 | tf_op jit(solution)/shard_map/exchange/pallas_call | solution.py:212
  20.0 14.5 %cross.1 = bf16[2,16,576,1152]{3,2,1,0:T(8,128)(2,1)} custom-call(f32[5,512,128]{2,1,0:T(8,128)S(1)} %get-tuple-element.7.mine_ref, f32[9,512,128]{2,1,0:T(8,128)S(1)} %get-tuple-element.8.every_ref), custom_call_target="tpu_custom_call" | custom-call | flops 1358954496 | bytes 42467328 | tf_op jit(solution)/shard_map/cross/pallas_call | solution.py:297

commit v4 on v3

--- a/solution.py
+++ b/solution.py
@@ -161,9 +161,10 @@
             white[:, w, :, 2 * low : 2 * high] = packed.reshape(count, local_bins, 2 * size)
         if c == 0:
             pl.semaphore_wait(barrier, count)
+        if c == n - 1:
+            send(0, near, 0, high)
         send(c, far, low, high)
     forward(0, white.at[me], me)
-    send(0, near, 0, samples_ref.shape[0])
 
     def settle(step):
         owner = peers[step]

time: 34.6 us -> 34.1 us (0.986)
  Pallas kernels: 34.4 us -> 34 us
    pallas_call x1, Pallas kernels: 19.9 us -> 19.5 us  [exchange(): pl.pallas_call(functools.partial(exchange_kernel, count), out_shape=(jax....]
where the time goes in v4:
time: 34.1 us; the launch traced here: 34 us
  Pallas kernels  34 us (100%)
    pallas_call x1, Pallas kernels, exchange(): pl.pallas_call(functools.partial(exchange_kernel, count), out_shape=(jax....  19.5 us
    pallas_call x1, Pallas kernels, cross(): pl.pallas_call(cross_kernel, grid=(steps,), out_shape=jax.ShapeDtypeStruc...  14.5 us

profile of v4, /device:TPU:1, one launch (start us, length us, event | category | flops | bytes accessed | tf_op | source)
XLA Modules:
  0.0 34.0 jit_solution(4337700969720754156)
XLA Ops:
  0.0 19.5 %exchange.1 = (f32[5,512,128]{2,1,0:T(8,128)S(1)}, f32[9,512,128]{2,1,0:T(8,128)S(1)}) custom-call(bf16[576,2,1024]{2,1,0:T(2,128)(2,1)} %samples_ref.1, bf16[1024,256]{1,0:T(8,128)(2,1)} %constant.4.table_ref), custom_call_target="tpu_custom_call" | custom-call | flops 603979776 | bytes 2359296 | tf_op jit(solution)/shard_map/exchange/pallas_call | solution.py:213
  19.5 14.5 %cross.1 = bf16[2,16,576,1152]{3,2,1,0:T(8,128)(2,1)} custom-call(f32[5,512,128]{2,1,0:T(8,128)S(1)} %get-tuple-element.7.mine_ref, f32[9,512,128]{2,1,0:T(8,128)S(1)} %get-tuple-element.8.every_ref), custom_call_target="tpu_custom_call" | custom-call | flops 1358954496 | bytes 42467328 | tf_op jit(solution)/shard_map/cross/pallas_call | solution.py:298
